TPU v7x, 32 devices: a whole 2x2x4 slice. The times are simulated.
32 devices in a mesh: parts: 2 (over y), tm: 4 (over z), factor: 4 (over x, core).
Axes of the slice: x: 2, y: 2, z: 4, core: 2. Of those that a mesh axis runs over, the one named last changes fastest.
Arguments:
- schur_matrix: float32 [24576, 24, 4, 128], P(('parts', 'tm'), None, 'factor'), parts along dimension 0, as said below
- link_rhs: float32 [24576], P(('parts', 'tm')), parts along dimension 0, may hold values from -6 to 6
- hour_rhs: float32 [32, 256], P(('parts', 'tm', 'factor')), parts along dimension 0, may hold values from -6 to 6
- link_cols: int32 [32, 256], P(('parts', 'tm', 'factor')), parts along dimension 0, may hold values from 0 to 255
- link_coef: float32 [32, 256], P(('parts', 'tm', 'factor')), parts along dimension 0, may hold values from -6 to 6
- hour_inverse: float32 [32, 256, 256], P(('parts', 'tm', 'factor')), parts along dimension 0, may hold values from -0.375 to 0.375
- couple_prev: float32 [32, 2, 256], P(('parts', 'tm', 'factor')), parts along dimension 0, may hold values from -1.2 to 1.2
- couple_next: float32 [32, 2, 256], P(('parts', 'tm', 'factor')), parts along dimension 0, may hold values from -1.2 to 1.2
Outputs:
- schur_trail: float32 [24576, 24, 4, 128], P(('parts', 'tm'), None, 'factor'), parts along dimension 0
- link_trail: float32 [24576], P(('parts', 'tm')), parts along dimension 0
- hour_step: float32 [32, 256], P(('parts', 'tm', 'factor')), parts along dimension 0
There are 2 independent parts, one for each index of `parts`. A program takes and returns all parts, laid end to end along the dimension named above; each array names one. Nothing has to cross between parts.
Inputs may be any that keep to these rules, and one draw needn't show every extreme that they name: schur_matrix is symmetric and its leading 2 * 128 rows and columns form a positive definite block.
All inputs are finite; a program needn't handle non-finite values.
Results may differ from a plain program's by a relative error of at most 0.0001.
Values sent between devices are 32-bit elements; how exact they have to be, the bound alone decides.
A program may use at most 192 MiB of HBM per device.

v0:
```python
import jax
import jax.numpy as jnp
from jax import lax
from jax.sharding import PartitionSpec as P

PANELS = 2
BW = 2
SWEEPS = 2


def spread(array, axis, root):
    mine = lax.axis_index(axis) == root
    return lax.psum(jnp.where(mine, array, jnp.zeros_like(array)), axis)


def with_halo(cells, sides, width):
    for axis, dim in sides:
        count = lax.axis_size(axis)
        ends = count - 1
        head = lax.slice_in_dim(cells, 0, width, axis=dim)
        tail = lax.slice_in_dim(cells, cells.shape[dim] - width, cells.shape[dim], axis=dim)
        cells = jnp.concatenate(
            [
                lax.ppermute(tail, axis, [(i, (i + 1) % count) for i in range(ends)]),
                cells,
                lax.ppermute(head, axis, [((i + 1) % count, i) for i in range(ends)]),
            ],
            axis=dim,
        )
    return cells


def shards(
    schur_matrix, link_rhs, hour_rhs, link_cols, link_coef, hour_inverse, couple_prev, couple_next
):
    rows_here = schur_matrix.shape[0]
    tiles_here = schur_matrix.shape[1]
    width = schur_matrix.shape[3]
    factors = lax.axis_size("factor")
    row_start = lax.axis_index("tm") * rows_here
    global_rows = row_start + jnp.arange(rows_here, dtype=jnp.int32)
    factor_here = lax.axis_index("factor")
    schur_now = schur_matrix
    rhs_now = link_rhs
    solved = []
    for panel_id in range(PANELS):
        column_tile = panel_id // factors
        owner_index = panel_id % factors
        own_cols = schur_now[:, column_tile, 0, :]
        panel_cols = spread(own_cols, "factor", owner_index)
        panel_first = panel_id * width
        picker = (
            global_rows[:, None] - panel_first == jnp.arange(width, dtype=jnp.int32)[None, :]
        ).astype(jnp.float32)
        block_part = jnp.dot(picker.T, panel_cols, precision=lax.Precision.HIGHEST)
        rhs_part = jnp.dot(picker.T, rhs_now, precision=lax.Precision.HIGHEST)
        diag_block, rhs_segment = lax.psum((block_part, rhs_part), "tm")
        lower_block = jnp.linalg.cholesky(diag_block)
        factor_rows = jax.scipy.linalg.solve_triangular(lower_block, panel_cols.T, lower=True).T
        factor_rows = jnp.where(
            (global_rows < panel_first)[:, None], jnp.zeros_like(factor_rows), factor_rows
        )
        all_factor = lax.all_gather(factor_rows, "tm", axis=0, tiled=True)
        grouped = all_factor.reshape(tiles_here, factors, width, width)
        my_tiles = lax.dynamic_index_in_dim(grouped, factor_here, 1, keepdims=False)
        link_step = jax.scipy.linalg.solve_triangular(lower_block, rhs_segment, lower=True)
        rhs_now = rhs_now - jnp.dot(factor_rows, link_step, precision=lax.Precision.HIGHEST)
        update = jnp.einsum("rk,tck->rtc", factor_rows, my_tiles, precision=lax.Precision.HIGHEST)
        schur_now = schur_now - update[:, :, None, :]
        solved.append(link_step)
    link_values = jnp.concatenate(solved)
    one_hot = (
        link_cols[:, :, None] == jnp.arange(PANELS * width, dtype=jnp.int32)[None, None, :]
    ).astype(jnp.float32)
    looked = jnp.einsum("hik,k->hi", one_hot, link_values, precision=lax.Precision.HIGHEST)
    target = hour_rhs - link_coef * looked
    hour_state = jnp.einsum("hik,hk->hi", hour_inverse, target, precision=lax.Precision.HIGHEST)
    for sweep_id in range(SWEEPS):
        border_pairs = jnp.concatenate((hour_state[:, :BW], hour_state[:, -BW:]), axis=1)
        padded = with_halo(border_pairs, ((("tm", "factor"), 0),), 1)
        prev_last = padded[:-2, BW:]
        next_first = padded[2:, :BW]
        coupling = jnp.einsum("hbi,hb->hi", couple_prev, prev_last, precision=lax.Precision.HIGHEST)
        coupling = coupling + jnp.einsum(
            "hbi,hb->hi", couple_next, next_first, precision=lax.Precision.HIGHEST
        )
        hour_state = jnp.einsum(
            "hik,hk->hi", hour_inverse, target - coupling, precision=lax.Precision.HIGHEST
        )
    return (schur_now, rhs_now, hour_state)


def solution(mesh):
    placed = (
        P(("parts", "tm"), None, "factor", None),
        P(("parts", "tm")),
        P(("parts", "tm", "factor"), None),
        P(("parts", "tm", "factor"), None),
        P(("parts", "tm", "factor"), None),
        P(("parts", "tm", "factor"), None, None),
        P(("parts", "tm", "factor"), None, None),
        P(("parts", "tm", "factor"), None, None),
    )
    return jax.shard_map(
        shards,
        mesh=mesh,
        in_specs=placed,
        out_specs=(
            P(("parts", "tm"), None, "factor", None),
            P(("parts", "tm")),
            P(("parts", "tm", "factor"), None),
        ),
        check_vma=False,
    )
```

profile of v0, /device:TPU:0, one launch (start us, length us, event | category | flops | bytes accessed | tf_op | source)
XLA Modules:
  0.0 661.5 jit_solution(964721345408237185)
XLA Ops:
  7.2 32.9 %copy.16 = f32[3072,24,1,128]{3,0,1,2:T(8,128)} copy(f32[3072,24,1,128]{3,2,1,0:T(1,128)} %param.13) | data formatting | bytes 75497472 | tf_op args[0]
  42.9 45.6 %all-reduce.5.cloned.1.call-done = f32[3072,128]{1,0:T(8,128)} async-done(((f32[3072,128]{1,0:T(8,128)}), f32[3072,128]{1,0:T(8,128)}) %all-reduce.5.cloned.1.call-update) | async-done | bytes 1572880 | tf_op jit(solution)/shard_map/psum | solution.py:13
  88.6 4.0 fusion.8
  92.6 34.1 %all-reduce.7.cloned.1.call-done = f32[128,128]{0,1:T(8,128)} async-done(((f32[128,128]{0,1:T(8,128)}), f32[128,128]{0,1:T(8,128)}) %all-reduce.7.cloned.1.call-update) | async-done | bytes 65552 | tf_op jit(solution)/shard_map/psum | solution.py:57
  128.6 11.7 %cholesky.44 = f32[128,128]{1,0:T(8,128)S(1)} custom-call(f32[128,128]{1,0:T(8,128)S(1)} %fusion.35), custom_call_target="Cholesky" | custom-call | tf_op jit(solution)/shard_map/jit(cholesky)/cholesky | solution.py:58
  141.6 9.8 %custom-call.10 = f32[1,128,128]{1,2,0:T(8,128)S(1)} custom-call(f32[1,128,128]{2,1,0:T(8,128)S(1)} %fusion.26), custom_call_target="InvertDiagBlocksLowerTriangular" | custom-call | tf_op jit(solution)/shard_map/jit(_solve_triangular)/triangular_solve | solution.py:59
  154.7 114.7 %all-gather.3.cloned.1.call-done = f32[12288,128]{0,1:T(8,128)} async-done(((f32[3072,128]{0,1:T(8,128)}), f32[12288,128]{0,1:T(8,128)}) %all-gather.3.cloned.1.call-update) | async-done | bytes 6291472 | tf_op jit(solution)/shard_map/all_gather | solution.py:63
  269.3 8.3 %reshape.109 = f32[24,4,128,128]{2,1,0,3:T(4,128)} reshape(f32[12288,128]{0,1:T(8,128)} %all-gather.3.cloned.1.call-done) | data formatting | bytes 12582912 | tf_op jit(solution)/shard_map/reshape | solution.py:64
  277.7 5.6 constant_dynamic-slice_fusion.1
  283.2 3.8 copy.14
  287.1 41.2 %bitcast_subtract_fusion.1 = f32[3072,24,1,128]{3,0,1,2:T(8,128)} fusion(f32[24,1,128,128]{3,2,0,1:T(8,128)S(1)} %copy.14, f32[128,3072]{1,0:T(8,128)S(1)} %copy-done.3, f32[3072,24,1,128]{3,2,1,0:T(1,128)} %param.13), kind=kOutput, calls=%fused_computation.1 | convolution fusion | flops 14504951808 | bytes 78643200 | tf_op jit(solution)/shard_map/rk,tck->rtc/dot_general | solution.py:68
  331.1 41.1 %all-reduce.9.cloned.1.call-done = f32[3072,128]{1,0:T(8,128)} async-done(((f32[3072,128]{1,0:T(8,128)}), f32[3072,128]{1,0:T(8,128)}) %all-reduce.9.cloned.1.call-update) | async-done | bytes 1572880 | tf_op jit(solution)/shard_map/psum | solution.py:13
  372.2 4.0 fusion.9
  376.5 34.0 %all-reduce.11.cloned.1.call-done = f32[128,128]{0,1:T(8,128)} async-done(((f32[128,128]{0,1:T(8,128)}), f32[128,128]{0,1:T(8,128)}) %all-reduce.11.cloned.1.call-update) | async-done | bytes 65552 | tf_op jit(solution)/shard_map/psum | solution.py:57
  412.9 12.5 %cholesky.55 = f32[128,128]{1,0:T(8,128)S(1)} custom-call(f32[128,128]{1,0:T(8,128)} %fusion.31), custom_call_target="Cholesky" | custom-call | tf_op jit(solution)/shard_map/jit(cholesky)/cholesky | solution.py:58
  427.4 10.6 %custom-call.11 = f32[1,128,128]{1,2,0:T(8,128)S(1)} custom-call(f32[1,128,128]{2,1,0:T(8,128)} %fusion.27), custom_call_target="InvertDiagBlocksLowerTriangular" | custom-call | tf_op jit(solution)/shard_map/jit(_solve_triangular)/triangular_solve | solution.py:59
  442.9 10.7 %psum.46 = f32[128]{0:T(128)S(1)} all-reduce(f32[128]{0:T(128)} %fusion.14), channel_id=1, replica_groups=mesh['parts'=2,'tm'=4,'factor'=4] {'tm'}, use_global_device_ids=true, to_apply=%region_6.9 | all-reduce | flops 128 | bytes 1024 | tf_op jit(solution)/shard_map/psum | solution.py:57
  456.9 8.7 %psum.47 = f32[128]{0:T(128)S(1)} all-reduce(f32[128]{0:T(128)S(1)} %fusion.13), channel_id=1, replica_groups=mesh['parts'=2,'tm'=4,'factor'=4] {'tm'}, use_global_device_ids=true, to_apply=%region_7.11 | all-reduce | flops 128 | bytes 1024 | tf_op jit(solution)/shard_map/psum | solution.py:57
  475.3 3.9 collective-permute-start.2
  480.9 75.3 %all-gather.5.cloned.1.call-done = f32[12288,128]{0,1:T(8,128)} async-done(((f32[3072,128]{0,1:T(8,128)}), f32[12288,128]{0,1:T(8,128)}) %all-gather.5.cloned.1.call-update) | async-done | bytes 6291472 | tf_op jit(solution)/shard_map/all_gather | solution.py:63
  556.2 8.3 %reshape.110 = f32[24,4,128,128]{2,1,0,3:T(4,128)} reshape(f32[12288,128]{0,1:T(8,128)} %all-gather.5.cloned.1.call-done) | data formatting | bytes 12582912 | tf_op jit(solution)/shard_map/reshape | solution.py:64
  564.5 5.6 constant_dynamic-slice_fusion
  573.8 37.3 %bitcast_subtract_fusion = f32[3072,24,1,128]{3,0,1,2:T(8,128)} fusion(f32[3072,24,1,128]{3,0,1,2:T(8,128)} %bitcast_subtract_fusion.1, f32[24,1,128,128]{3,2,0,1:T(8,128)S(1)} %copy.19, f32[128,3072]{1,0:T(8,128)S(1)} %copy-done.2), kind=kOutput, calls=%fused_computation | convolution fusion | flops 14504951808 | bytes 78643200 | tf_op jit(solution)/shard_map/rk,tck->rtc/dot_general | solution.py:68
  611.1 43.3 %copy.21 = f32[3072,24,1,128]{3,2,1,0:T(1,128)} copy(f32[3072,24,1,128]{3,0,1,2:T(8,128)} %bitcast_subtract_fusion) | data formatting | bytes 75497472
  (81 shorter events, 39.6 us)
Async XLA Ops:
  7.2 459.6 %copy-start = (f32[1,256,256]{2,1,0:T(8,128)S(1)}, f32[1,256,256]{2,1,0:T(8,128)}, u32[]{:S(2)}) copy-start(f32[1,256,256]{2,1,0:T(8,128)} %param.18) | copy-start | bytes 786436
  7.2 81.4 %all-reduce.5.cloned.1.call-start = ((), (), s32[]{:S(2)}) async-start(), calls=%async_computation | async-start | bytes 3145728 | tf_op jit(solution)/shard_map/psum | solution.py:13
  42.9 83.9 %all-reduce.7.cloned.1.call-start = ((), (), s32[]{:S(2)}) async-start(), calls=%async_computation.1 | async-start | bytes 131072 | tf_op jit(solution)/shard_map/psum | solution.py:57
  88.6 62.9 %copy-start.4 = (f32[3072,128]{1,0:T(8,128)S(1)}, f32[3072,128]{1,0:T(8,128)}, u32[]{:S(2)}) copy-start(f32[3072,128]{1,0:T(8,128)} %all-reduce.5.cloned.1.call-done) | copy-start | bytes 4718596
  92.6 176.8 %all-gather.3.cloned.1.call-start = ((), (), s32[]{:S(2)}) async-start(), calls=%async_computation.2 | async-start | bytes 7864320 | tf_op jit(solution)/shard_map/all_gather | solution.py:63
  154.1 218.1 %all-reduce.9.cloned.1.call-start = ((), (), s32[]{:S(2)}) async-start(), calls=%async_computation.3 | async-start | bytes 3145728 | tf_op jit(solution)/shard_map/psum | solution.py:13
  283.2 3.9 copy-start.3
  331.0 79.4 %all-reduce.11.cloned.1.call-start = ((), (), s32[]{:S(2)}) async-start(), calls=%async_computation.4 | async-start | bytes 131072 | tf_op jit(solution)/shard_map/psum | solution.py:57
  331.1 45.4 %copy-start.6 = (s32[3072]{0:T(1024)}, s32[3072]{0:T(1024)S(1)}, u32[]{:S(2)}) copy-start(s32[3072]{0:T(1024)S(1)} %fusion.36) | copy-start | bytes 36868
  372.2 65.8 %copy-start.5 = (f32[3072,128]{1,0:T(8,128)S(1)}, f32[3072,128]{1,0:T(8,128)}, u32[]{:S(2)}) copy-start(f32[3072,128]{1,0:T(8,128)} %all-reduce.9.cloned.1.call-done) | copy-start | bytes 4718596
  376.2 180.0 %all-gather.5.cloned.1.call-start = ((), (), s32[]{:S(2)}) async-start(), calls=%async_computation.5 | async-start | bytes 7864320 | tf_op jit(solution)/shard_map/all_gather | solution.py:63
  440.7 25.0 %copy-start.9 = (f32[1,256]{1,0:T(1,128)S(1)}, f32[1,256]{1,0:T(1,128)}, u32[]{:S(2)}) copy-start(f32[1,256]{1,0:T(1,128)} %param.15) | copy-start | bytes 3076
  440.7 30.9 %copy-start.2 = (f32[128,3072]{1,0:T(8,128)S(1)}, f32[128,3072]{1,0:T(8,128)}, u32[]{:S(2)}) copy-start(f32[128,3072]{1,0:T(8,128)} %convolution_select_fusion) | copy-start | bytes 4718596
  454.7 18.5 %copy-start.7 = (f32[1,2,256]{2,1,0:T(2,128)S(1)}, f32[1,2,256]{2,1,0:T(2,128)}, u32[]{:S(2)}) copy-start(f32[1,2,256]{2,1,0:T(2,128)} %param.20) | copy-start | bytes 6148
  454.7 18.6 %copy-start.8 = (f32[1,2,256]{2,1,0:T(2,128)S(1)}, f32[1,2,256]{2,1,0:T(2,128)}, u32[]{:S(2)}) copy-start(f32[1,2,256]{2,1,0:T(2,128)} %param.19) | copy-start | bytes 6148
  467.3 5.9 collective-permute-start.1
  468.6 4.7 collective-permute-start
  474.0 5.2 collective-permute-start.3
  475.3 4.5 collective-permute-start.2
  611.1 43.3 %copy-start.1 = (f32[1,256,256]{2,1,0:T(8,128)S(1)}, f32[1,256,256]{2,1,0:T(8,128)}, u32[]{:S(2)}) copy-start(f32[1,256,256]{2,1,0:T(8,128)} %param.18) | copy-start | bytes 786436
Sparse Core Ops, SparseCore 0:
  43.0 45.5 all-reduce.4
  92.7 34.0 all-reduce.6
  154.3 115.0 all-gather.2
  331.1 41.0 all-reduce.8
  376.4 34.0 all-reduce.10
  440.8 115.3 all-gather.4
where the time goes:
time: 671 us; the launch traced here: 662 us
  waiting for transfers between devices  345 us (51%)
  local copies, waits for them, and re-layouts  114 us (17%)
  matrix products  101 us (15%)
  other arithmetic  57.2 us (9%)
  blocking collectives  19.4 us (3%)
  between operations  14.7 us (2%)
  starting transfers between devices  10.4 us (2%)
    all_gather x2, waiting for transfers between devices, shards(): all_factor = lax.all_gather(factor_rows, 'tm', axis=0, tiled=True)  190 us
    psum x2, waiting for transfers between devices, spread(): return lax.psum(jnp.where(mine, array, jnp.zeros_like(array)), axis)  86.8 us
    dot_general x2, matrix products, shards(): jnp.einsum('rk,tck->rtc', factor_rows, my_tiles, precision=lax.Precision....  78.5 us
    unnamed x22, local copies, waits for them, and re-layouts  76.3 us
    psum x2, waiting for transfers between devices, shards(): diag_block, rhs_segment = lax.psum((block_part, rhs_part), 'tm')  68.1 us
    another operation x6, other arithmetic, shards(): lower_block = jnp.linalg.cholesky(diag_block)  25.6 us
    another operation x4, other arithmetic, shards(): jax.scipy.linalg.solve_triangular(lower_block, panel_cols.T, lower=True)  22.4 us
    psum x2, blocking collectives, shards(): diag_block, rhs_segment = lax.psum((block_part, rhs_part), 'tm')  19.4 us
  transfers between devices with their start and end apart: 10, of which 7 were waited for; matrix products, arithmetic and copies ran while one was open for 2% of the time, Pallas kernels for 0%

commit v1 on v0

--- a/solution.py
+++ b/solution.py
@@ -60,7 +60,15 @@
         factor_rows = jnp.where(
             (global_rows < panel_first)[:, None], jnp.zeros_like(factor_rows), factor_rows
         )
-        all_factor = lax.all_gather(factor_rows, "tm", axis=0, tiled=True)
+        ways, here = (lax.axis_size("tm"), lax.axis_index("tm"))
+        grown, reach = (factor_rows, 1)
+        while reach < ways:
+            theirs = lax.ppermute(grown, "tm", [(d, d ^ reach) for d in range(ways)])
+            mine_first = jnp.concatenate([grown, theirs], axis=0)
+            theirs_first = jnp.concatenate([theirs, grown], axis=0)
+            grown = jnp.where(here & reach == 0, mine_first, theirs_first)
+            reach = 2 * reach
+        all_factor = grown
         grouped = all_factor.reshape(tiles_here, factors, width, width)
         my_tiles = lax.dynamic_index_in_dim(grouped, factor_here, 1, keepdims=False)
         link_step = jax.scipy.linalg.solve_triangular(lower_block, rhs_segment, lower=True)

time: 671 us -> 819 us (1.22)
  the two profiles are of different devices: /device:TPU:0 before, /device:TPU:16 now
where the time goes in v1:
time: 819 us; the launch traced here: 814 us
  waiting for transfers between devices  328 us (40%)
  blocking collectives  170 us (21%)
  local copies, waits for them, and re-layouts  114 us (14%)
  matrix products  97 us (12%)
  other arithmetic  76.6 us (9%)
  starting transfers between devices  14.5 us (2%)
  between operations  14.3 us (2%)
    psum x2, blocking collectives, shards(): diag_block, rhs_segment = lax.psum((block_part, rhs_part), 'tm')  170 us
    ppermute x4, waiting for transfers between devices, shards(): theirs = lax.ppermute(grown, 'tm', [(d, d ^ reach) for d in range(ways)])  166 us
    psum x2, waiting for transfers between devices, spread(): return lax.psum(jnp.where(mine, array, jnp.zeros_like(array)), axis)  89.6 us
    dot_general x2, matrix products, shards(): jnp.einsum('rk,tck->rtc', factor_rows, my_tiles, precision=lax.Precision....  78.5 us
    unnamed x24, local copies, waits for them, and re-layouts  76.3 us
    psum x2, waiting for transfers between devices, shards(): diag_block, rhs_segment = lax.psum((block_part, rhs_part), 'tm')  67.5 us
    another operation x6, other arithmetic, shards(): lower_block = jnp.linalg.cholesky(diag_block)  24.8 us
    select_n x4, other arithmetic, shards(): grown = jnp.where(here & reach == 0, mine_first, theirs_first)  22.3 us
  transfers between devices with their start and end apart: 12, of which 8 were waited for; matrix products, arithmetic and copies ran while one was open for 1% of the time, Pallas kernels for 0%

profile of v1, /device:TPU:16, one launch (start us, length us, event | category | flops | bytes accessed | tf_op | source)
XLA Modules:
  0.0 814.3 jit_solution(361373015431380275)
XLA Ops:
  7.2 32.9 %copy.16 = f32[3072,24,1,128]{3,0,1,2:T(8,128)} copy(f32[3072,24,1,128]{3,2,1,0:T(1,128)} %param.13) | data formatting | bytes 75497472 | tf_op args[0]
  42.9 44.0 %all-reduce.5.cloned.1.call-done = f32[3072,128]{1,0:T(8,128)} async-done(((f32[3072,128]{1,0:T(8,128)}), f32[3072,128]{1,0:T(8,128)}) %all-reduce.5.cloned.1.call-update) | async-done | bytes 1572880 | tf_op jit(solution)/shard_map/psum | solution.py:13
  86.9 4.0 fusion.8
  91.3 33.6 %all-reduce.7.cloned.1.call-done = f32[128,128]{0,1:T(8,128)} async-done(((f32[128,128]{0,1:T(8,128)}), f32[128,128]{0,1:T(8,128)}) %all-reduce.7.cloned.1.call-update) | async-done | bytes 65552 | tf_op jit(solution)/shard_map/psum | solution.py:57
  126.7 11.7 %cholesky.44 = f32[128,128]{1,0:T(8,128)S(1)} custom-call(f32[128,128]{1,0:T(8,128)S(1)} %fusion.35), custom_call_target="Cholesky" | custom-call | tf_op jit(solution)/shard_map/jit(cholesky)/cholesky | solution.py:58
  139.7 9.8 %custom-call.10 = f32[1,128,128]{1,2,0:T(8,128)S(1)} custom-call(f32[1,128,128]{2,1,0:T(8,128)S(1)} %fusion.26), custom_call_target="InvertDiagBlocksLowerTriangular" | custom-call | tf_op jit(solution)/shard_map/jit(_solve_triangular)/triangular_solve | solution.py:59
  151.7 33.7 %collective-permute-done = f32[3072,128]{0,1:T(8,128)S(1)} collective-permute-done((f32[3072,128]{0,1:T(8,128)S(1)}, f32[3072,128]{0,1:T(8,128)S(1)}, u32[]{:S(2)}, u32[]{:S(2)}) %collective-permute-start) | collective-permute-done | bytes 1572896 | tf_op jit(solution)/shard_map/ppermute | solution.py:66
  188.1 132.2 %collective-permute-done.1 = f32[6144,128]{0,1:T(8,128)} collective-permute-done((f32[6144,128]{0,1:T(8,128)}, f32[6144,128]{0,1:T(8,128)}, u32[]{:S(2)}, u32[]{:S(2)}) %collective-permute-start.1) | collective-permute-done | bytes 3145760 | tf_op jit(solution)/shard_map/ppermute | solution.py:66
  320.3 8.5 %maximum_select_fusion = f32[12288,128]{0,1:T(8,128)} fusion(f32[6144,128]{0,1:T(8,128)} %collective-permute-done.1, f32[6144,128]{0,1:T(8,128)} %maximum_select_fusion.2, pred[]{:T(512)S(6)} %eq.76), kind=kLoop, calls=%fused_computation.2 | loop fusion | flops 4718592 | bytes 12582913 | tf_op jit(solution)/shard_map/jit(_where)/select_n | solution.py:69
  328.8 8.3 %select_n.82 = f32[24,4,128,128]{2,1,0,3:T(4,128)} reshape(f32[12288,128]{0,1:T(8,128)} %maximum_select_fusion) | data formatting | bytes 12582912 | tf_op jit(solution)/shard_map/jit(_where)/select_n | solution.py:69
  337.1 5.5 constant_dynamic-slice_fusion.1
  346.4 41.2 %bitcast_subtract_fusion.1 = f32[3072,24,1,128]{3,0,1,2:T(8,128)} fusion(f32[24,1,128,128]{3,2,0,1:T(8,128)S(1)} %copy.14, f32[128,3072]{1,0:T(8,128)S(1)} %convolution_select_fusion.1, f32[3072,24,1,128]{3,2,1,0:T(1,128)} %param.13), kind=kOutput, calls=%fused_computation.1 | convolution fusion | flops 14504951808 | bytes 78643200 | tf_op jit(solution)/shard_map/rk,tck->rtc/dot_general | solution.py:76
  390.6 45.6 %all-reduce.9.cloned.1.call-done = f32[3072,128]{1,0:T(8,128)} async-done(((f32[3072,128]{1,0:T(8,128)}), f32[3072,128]{1,0:T(8,128)}) %all-reduce.9.cloned.1.call-update) | async-done | bytes 1572880 | tf_op jit(solution)/shard_map/psum | solution.py:13
  440.1 33.9 %all-reduce.11.cloned.1.call-done = f32[128,128]{0,1:T(8,128)} async-done(((f32[128,128]{0,1:T(8,128)}), f32[128,128]{0,1:T(8,128)}) %all-reduce.11.cloned.1.call-update) | async-done | bytes 65552 | tf_op jit(solution)/shard_map/psum | solution.py:57
  475.8 11.7 %cholesky.55 = f32[128,128]{1,0:T(8,128)S(1)} custom-call(f32[128,128]{1,0:T(8,128)S(1)} %fusion.31), custom_call_target="Cholesky" | custom-call | tf_op jit(solution)/shard_map/jit(cholesky)/cholesky | solution.py:58
  488.8 9.8 %custom-call.11 = f32[1,128,128]{1,2,0:T(8,128)S(1)} custom-call(f32[1,128,128]{2,1,0:T(8,128)S(1)} %fusion.27), custom_call_target="InvertDiagBlocksLowerTriangular" | custom-call | tf_op jit(solution)/shard_map/jit(_solve_triangular)/triangular_solve | solution.py:59
  503.0 35.4 %psum.46 = f32[128]{0:T(128)S(1)} all-reduce(f32[128]{0:T(128)S(1)} %fusion.14), channel_id=1, replica_groups=mesh['parts'=2,'tm'=4,'factor'=4] {'tm'}, use_global_device_ids=true, to_apply=%region_6.9 | all-reduce | flops 128 | bytes 1024 | tf_op jit(solution)/shard_map/psum | solution.py:57
  540.2 3.9 maximum_select_fusion.3
  548.2 134.5 %psum.47 = f32[128]{0:T(128)S(1)} all-reduce(f32[128]{0:T(128)S(1)} %fusion.13), channel_id=1, replica_groups=mesh['parts'=2,'tm'=4,'factor'=4] {'tm'}, use_global_device_ids=true, to_apply=%region_7.11 | all-reduce | flops 128 | bytes 1024 | tf_op jit(solution)/shard_map/psum | solution.py:57
  701.4 7.9 maximum_select_fusion.1
  709.3 8.3 %select_n.91 = f32[24,4,128,128]{2,1,0,3:T(4,128)} reshape(f32[12288,128]{0,1:T(8,128)} %maximum_select_fusion.1) | data formatting | bytes 12582912 | tf_op jit(solution)/shard_map/jit(_where)/select_n | solution.py:69
  717.6 5.6 constant_dynamic-slice_fusion
  726.9 37.3 %bitcast_subtract_fusion = f32[3072,24,1,128]{3,0,1,2:T(8,128)} fusion(f32[3072,24,1,128]{3,0,1,2:T(8,128)} %bitcast_subtract_fusion.1, f32[24,1,128,128]{3,2,0,1:T(8,128)S(1)} %copy.19, f32[128,3072]{1,0:T(8,128)S(1)} %convolution_select_fusion), kind=kOutput, calls=%fused_computation | convolution fusion | flops 14504951808 | bytes 78643200 | tf_op jit(solution)/shard_map/rk,tck->rtc/dot_general | solution.py:76
  764.2 43.3 %copy.21 = f32[3072,24,1,128]{3,2,1,0:T(1,128)} copy(f32[3072,24,1,128]{3,0,1,2:T(8,128)} %bitcast_subtract_fusion) | data formatting | bytes 75497472
  (89 shorter events, 57.2 us)
Async XLA Ops:
  7.2 676.1 %copy-start = (f32[1,256,256]{2,1,0:T(8,128)S(1)}, f32[1,256,256]{2,1,0:T(8,128)}, u32[]{:S(2)}) copy-start(f32[1,256,256]{2,1,0:T(8,128)} %param.18) | copy-start | bytes 786436
  7.2 79.7 %all-reduce.5.cloned.1.call-start = ((), (), s32[]{:S(2)}) async-start(), calls=%async_computation | async-start | bytes 3145728 | tf_op jit(solution)/shard_map/psum | solution.py:13
  42.9 82.0 %all-reduce.7.cloned.1.call-start = ((), (), s32[]{:S(2)}) async-start(), calls=%async_computation.1 | async-start | bytes 131072 | tf_op jit(solution)/shard_map/psum | solution.py:57
  86.9 62.6 %copy-start.2 = (f32[3072,128]{1,0:T(8,128)S(1)}, f32[3072,128]{1,0:T(8,128)}, u32[]{:S(2)}) copy-start(f32[3072,128]{1,0:T(8,128)} %all-reduce.5.cloned.1.call-done) | copy-start | bytes 4718596
  91.0 345.2 %all-reduce.9.cloned.1.call-start = ((), (), s32[]{:S(2)}) async-start(), calls=%async_computation.2 | async-start | bytes 3145728 | tf_op jit(solution)/shard_map/psum | solution.py:13
  151.1 34.3 %collective-permute-start = (f32[3072,128]{0,1:T(8,128)S(1)}, f32[3072,128]{0,1:T(8,128)S(1)}, u32[]{:S(2)}, u32[]{:S(2)}) collective-permute-start(f32[3072,128]{0,1:T(8,128)S(1)} %bitcast.148), channel_id=1, source_target_pairs={{0,4},{4,0},{8,12},{12,8},{1,5},{5,1},{9,13},{13,9},{2,6},{6,2},{1... | collective-permute-start | bytes 4718600 | tf_op jit(solution)/shard_map/ppermute | solution.py:66
  187.3 132.9 %collective-permute-start.1 = (f32[6144,128]{0,1:T(8,128)}, f32[6144,128]{0,1:T(8,128)}, u32[]{:S(2)}, u32[]{:S(2)}) collective-permute-start(f32[6144,128]{0,1:T(8,128)} %maximum_select_fusion.2), channel_id=1, source_target_pairs={{0,8},{4,12},{8,0},{12,4},{1,9},{5,13},{9,1},{13,5},{2,10},{6,14},... | collective-permute-start | bytes 9437192 | tf_op jit(solution)/shard_map/ppermute | solution.py:66
  390.3 83.7 %all-reduce.11.cloned.1.call-start = ((), (), s32[]{:S(2)}) async-start(), calls=%async_computation.3 | async-start | bytes 131072 | tf_op jit(solution)/shard_map/psum | solution.py:57
  390.6 97.6 %copy-start.3 = (s32[3072]{0:T(1024)}, s32[3072]{0:T(1024)S(1)}, u32[]{:S(2)}) copy-start(s32[3072]{0:T(1024)S(1)} %fusion.36) | copy-start | bytes 36868
  498.7 3.6 copy-start.5
  501.6 38.6 %collective-permute-start.2 = (f32[3072,128]{0,1:T(8,128)S(1)}, f32[3072,128]{0,1:T(8,128)}, u32[]{:S(2)}, u32[]{:S(2)}) collective-permute-start(f32[3072,128]{0,1:T(8,128)S(1)} %bitcast.146), channel_id=1, source_target_pairs={{0,4},{4,0},{8,12},{12,8},{1,5},{5,1},{9,13},{13,9},{2,6},{6,2},{1... | collective-permute-start | bytes 4718600 | tf_op jit(solution)/shard_map/ppermute | solution.py:66
  540.2 7.2 copy-start.4
  540.2 142.7 %copy-start.8 = (f32[1,256]{1,0:T(1,128)S(1)}, f32[1,256]{1,0:T(1,128)}, u32[]{:S(2)}) copy-start(f32[1,256]{1,0:T(1,128)} %param.15) | copy-start | bytes 3076
  540.2 142.7 %copy-start.9 = (f32[1,256]{1,0:T(1,128)S(1)}, f32[1,256]{1,0:T(1,128)}, u32[]{:S(2)}) copy-start(f32[1,256]{1,0:T(1,128)} %param.17) | copy-start | bytes 3076
  540.2 142.7 %copy-start.10 = (s32[1,256]{1,0:T(1,128)S(1)}, s32[1,256]{1,0:T(1,128)}, u32[]{:S(2)}) copy-start(s32[1,256]{1,0:T(1,128)} %param.16) | copy-start | bytes 3076
  544.2 145.5 %copy-start.6 = (f32[1,2,256]{2,1,0:T(2,128)S(1)}, f32[1,2,256]{2,1,0:T(2,128)}, u32[]{:S(2)}) copy-start(f32[1,2,256]{2,1,0:T(2,128)} %param.20) | copy-start | bytes 6148
  544.2 147.3 %copy-start.7 = (f32[1,2,256]{2,1,0:T(2,128)S(1)}, f32[1,2,256]{2,1,0:T(2,128)}, u32[]{:S(2)}) copy-start(f32[1,2,256]{2,1,0:T(2,128)} %param.19) | copy-start | bytes 6148
  544.2 157.2 %collective-permute-start.3 = (f32[6144,128]{0,1:T(8,128)}, f32[6144,128]{0,1:T(8,128)}, u32[]{:S(2)}, u32[]{:S(2)}) collective-permute-start(f32[6144,128]{0,1:T(8,128)} %maximum_select_fusion.3), channel_id=1, source_target_pairs={{0,8},{4,12},{8,0},{12,4},{1,9},{5,13},{9,1},{13,5},{2,10},{6,14},... | collective-permute-start | bytes 9437192 | tf_op jit(solution)/shard_map/ppermute | solution.py:66
  683.8 5.9 collective-permute-start.5
  685.7 5.8 collective-permute-start.4
  692.1 4.3 collective-permute-start.7
  694.5 5.8 collective-permute-start.6
  764.2 43.3 %copy-start.1 = (f32[1,256,256]{2,1,0:T(8,128)S(1)}, f32[1,256,256]{2,1,0:T(8,128)}, u32[]{:S(2)}) copy-start(f32[1,256,256]{2,1,0:T(8,128)} %param.18) | copy-start | bytes 786436
Sparse Core Ops, SparseCore 0:
  43.0 43.9 all-reduce.4
  91.1 33.7 all-reduce.6
  390.4 45.7 all-reduce.8
  440.2 33.7 all-reduce.10
